TPU v7x, 256 devices: a whole 4x4x8 slice. The times are simulated.
256 devices in a mesh: row: 16 (over z, core), col: 16 (over x, y).
Axes of the slice: x: 4, y: 4, z: 8, core: 2. Of those that a mesh axis runs over, the one named last changes fastest.
Arguments:
- panels: bfloat16 [2, 16384, 512], P(None, 'row'), may hold values from -2 to 2
- row_pattern: int32 [2, 128], replicated, may hold values from 0 to 1, as said below
- coupling: bfloat16 [512, 512], P('row'), may hold values from -0.3125 to 0.3125
- inverse_factors: bfloat16 [2, 512, 512], replicated, as said below
- trailing: float32 [16384, 16384], P('row', 'col'), may hold values from -6 to 6
Outputs:
- factor: bfloat16 [2, 16384, 512], P(None, 'row')
- updated: float32 [16384, 16384], P('row', 'col')
Inputs may be any that keep to these rules, and one draw needn't show every extreme that they name: `row_pattern`: in each panel, the 8 entries of every aligned block (the tile rows of one index of row) hold 1 to 3 ones, and some block of each panel holds exactly 3. `inverse_factors`: each block is lower triangular with a positive diagonal.
All inputs are finite; a program needn't handle non-finite values.
Results may differ from a plain program's by a relative error of at most 0.0023.
Values may be sent and summed in bfloat16 or wider, within the bound.
A program may use at most 64 MiB of HBM per device.

v0:
```python
import jax
import jax.numpy as jnp
from jax import lax
from jax.sharding import PartitionSpec as P

W = 512
BS = 128
TR_DEV = 8


def spread(block, axis, source):
    block = jnp.where(lax.axis_index(axis) == source, block, jnp.zeros_like(block))
    return lax.psum(block, axis)


def masked(values, present_mask):
    shaped = values.reshape(TR_DEV, BS, W) * present_mask[:, None, None]
    return shaped.reshape(TR_DEV * BS, W)


def sender_pattern(row_pattern, sender):
    return lax.dynamic_slice_in_dim(row_pattern, sender * TR_DEV, TR_DEV, 1)


def body(panels, row_pattern, coupling, inverse_factors, trailing):
    col_count = lax.axis_size("col")
    row_ratio = lax.axis_size("row") // col_count
    col_index = lax.axis_index("col")
    own_pattern = sender_pattern(row_pattern, lax.axis_index("row"))
    own_mask = own_pattern.astype(jnp.float32)
    first_inverse = inverse_factors[0]
    second_inverse = inverse_factors[1]
    first_factor = masked(
        jnp.einsum("rw,vw->rv", panels[0], first_inverse, preferred_element_type=jnp.float32),
        own_mask[0],
    ).astype(jnp.bfloat16)
    coupled_part = jnp.einsum(
        "rw,vw->rv", coupling, first_inverse, preferred_element_type=jnp.float32
    ).astype(jnp.bfloat16)
    coupled = lax.all_gather(coupled_part, "row", axis=0, tiled=True)
    second_input = panels[1].astype(jnp.float32) - jnp.einsum(
        "rw,vw->rv", first_factor, coupled, preferred_element_type=jnp.float32
    )
    second_product = jnp.dot(
        second_input, second_inverse.astype(jnp.float32).T, precision=lax.Precision.HIGHEST
    )
    second_factor = masked(second_product, own_mask[1]).astype(jnp.bfloat16)
    factor = jnp.stack((first_factor, second_factor))
    sender = col_index + 0
    received = [spread(factor, "row", sender)]
    stacked = jnp.stack(received).reshape(row_ratio, 2, TR_DEV, BS, W)
    update = jnp.einsum(
        "krw,qklcw->rlqc", factor, stacked, preferred_element_type=jnp.float32
    ).reshape(trailing.shape)
    result = trailing - update
    return (factor, result)


def solution(mesh):
    placed = (P(None, "row", None), P(), P("row", None), P(), P("row", "col"))
    return jax.shard_map(
        body,
        mesh=mesh,
        in_specs=placed,
        out_specs=(P(None, "row", None), P("row", "col")),
        check_vma=False,
    )
```

profile of v0, /device:TPU:71, one launch (start us, length us, event | category | flops | bytes accessed | tf_op | source)
XLA Modules:
  0.0 173.0 jit_solution(5943475332292541484)
XLA Ops:
  7.2 0.0 copy-start
  7.2 0.0 copy-start.3
  7.2 0.0 slice-start
  7.2 0.0 all-reduce.2.cloned.1.call-start
  7.3 0.9 dynamic-slice_convert_fusion
  8.2 0.0 copy-done
  8.2 1.3 convolution_convert_fusion
  9.4 18.9 %all_gather.3 = bf16[512,512]{1,0:T(8,128)(2,1)S(1)} all-gather(bf16[32,512]{1,0:T(8,128)(2,1)S(1)} %convolution_convert_fusion), channel_id=1, replica_groups=mesh['row'=16,'col'=16] {'row'}, dimensions={0}, use_global_device_ids=true | all-gather | bytes 557056 | tf_op jit(solution)/shard_map/all_gather | solution.py:40
  28.3 0.0 copy-start.2
  28.3 0.0 copy-done.3
  28.4 0.0 slice-done
  28.4 0.7 multiply_convert_fusion.1
  29.1 0.8 copy-done.2
  29.9 0.7 convert_subtract_fusion
  30.7 1.8 %multiply_convert_fusion = bf16[8,128,512]{2,1,0:T(8,128)(2,1)S(1)} fusion(f32[8,128,512]{2,1,0:T(8,128)S(1)} %bitcast.40, f32[8]{0:T(128)S(1)} %get-tuple-element.4, bf16[2,512,512]{2,1,0:T(8,128)(2,1)S(1)} %copy-done.3), kind=kOutput, calls=%fused_computation.4 | convolution fusion | flops 3222274048 | bytes 3670528 | tf_op jit(solution)/shard_map/dot_general | solution.py:44
  32.5 0.3 broadcast_select_fusion
  32.8 0.0 copy-start.1
  32.8 1.7 copy.7
  34.5 0.0 all-reduce.2.cloned.1.call-update
  34.5 113.5 %all-reduce.2.cloned.1.call-done = bf16[2,8,128,512]{3,2,0,1:T(8,128)(2,1)} async-done(((bf16[2,8,128,512]{3,2,0,1:T(8,128)(2,1)}), bf16[2,8,128,512]{3,2,0,1:T(8,128)(2,1)}) %all-reduce.2.cloned.1.call-update) | async-done | bytes 2097168 | tf_op jit(solution)/shard_map/psum | solution.py:13
  148.0 0.0 copy-done.1
  148.0 6.0 %fusion = f32[8,128,1024,1]{2,1,3,0:T(8,128)} fusion(bf16[2,8,128,512]{3,2,0,1:T(8,128)(2,1)} %all-reduce.2.cloned.1.call-done, bf16[2,1024,512]{2,1,0:T(8,128)(2,1)S(1)} %get-tuple-element.3), kind=kOutput, calls=%fused_computation.2 | convolution fusion | flops 2147483648 | bytes 8388608 | tf_op jit(solution)/shard_map/krw,qklcw->rlqc/dot_general | solution.py:52
  154.0 5.3 %copy.8 = f32[1024,1024]{1,0:T(8,128)} copy(f32[1024,1024]{0,1:T(8,128)} %bitcast.41) | data formatting | bytes 8388608 | tf_op jit(solution)/shard_map/reshape | solution.py:54
  159.3 6.8 %sub.7 = f32[1024,1024]{1,0:T(8,128)} subtract(f32[1024,1024]{1,0:T(8,128)} %param.9, f32[1024,1024]{1,0:T(8,128)} %copy.8) | non-fusion elementwise | flops 1048576 | bytes 12582912 | tf_op jit(solution)/shard_map/sub | solution.py:55
  (1 shorter events, 0.0 us)
Async XLA Ops:
  7.2 1.0 copy-start
  7.2 21.2 %copy-start.3 = (bf16[2,512,512]{2,1,0:T(8,128)(2,1)S(1)}, bf16[2,512,512]{2,1,0:T(8,128)(2,1)}, u32[]{:S(2)}) copy-start(bf16[2,512,512]{2,1,0:T(8,128)(2,1)} %param.8) | copy-start | bytes 3145732
  7.2 21.2 %slice-start = ((bf16[2,1024,512]{2,1,0:T(8,128)(2,1)}), bf16[1,1024,512]{2,1,0:T(8,128)(2,1)S(1)}, s32[]{:S(2)}) async-start(bf16[2,1024,512]{2,1,0:T(8,128)(2,1)} %param.5), calls=%async_computation.1 | async-start | bytes 2097152 | tf_op jit(solution)/shard_map/slice | solution.py:34
  7.2 140.8 %all-reduce.2.cloned.1.call-start = ((), (), s32[]{:S(2)}) async-start(), calls=%async_computation | async-start | bytes 4194304 | tf_op jit(solution)/shard_map/psum | solution.py:13
  28.3 1.6 copy-start.2
  32.8 115.2 %copy-start.1 = (bf16[2,1024,512]{2,1,0:T(8,128)(2,1)}, bf16[2,1024,512]{2,1,0:T(8,128)(2,1)S(1)}, u32[]{:S(2)}) copy-start(bf16[2,1024,512]{2,1,0:T(8,128)(2,1)S(1)} %get-tuple-element.3) | copy-start | bytes 6291460
Sparse Core Ops, SparseCore 0:
  34.6 113.3 all-reduce.1
where the time goes:
time: 176 us; the launch traced here: 173 us
  waiting for transfers between devices  114 us (65%)
  blocking collectives  18.9 us (11%)
  between operations  14.1 us (8%)
  matrix products  10.6 us (6%)
  other arithmetic  8.01 us (5%)
  local copies, waits for them, and re-layouts  7.89 us (4%)
    psum x1, waiting for transfers between devices, spread(): return lax.psum(block, axis)  114 us
    all_gather x1, blocking collectives, body(): coupled = lax.all_gather(coupled_part, 'row', axis=0, tiled=True)  18.9 us
    sub x1, other arithmetic, body(): result = trailing - update  6.85 us
    dot_general x1, matrix products, body(): jnp.einsum('krw,qklcw->rlqc', factor, stacked, preferred_element_type=jnp...  5.96 us
    reshape x1, local copies, waits for them, and re-layouts, body(): update = jnp.einsum('krw,qklcw->rlqc', factor, stacked, preferred_element...  5.35 us
  transfers between devices with their start and end apart: 1, of which 1 were waited for; matrix products, arithmetic and copies ran while one was open for 0% of the time, Pallas kernels for 0%

commit v1 on v0

v1 whole, which is shorter than its diff:
```python
import jax
import jax.numpy as jnp
from jax import lax
from jax.experimental import pallas as pl
from jax.experimental.pallas import tpu as pltpu
from jax.sharding import PartitionSpec as P

W = 512
BS = 128
TR = 8
PMAX = 3
NZ = 8
NP = 16
MESH = pl.DeviceIdType.MESH
BF = jnp.bfloat16
F32 = jnp.float32


def dot_t(a, b):
    return lax.dot_general(a, b, (((1,), (1,)), ((), ())), preferred_element_type=F32)


def places(pattern, panel, block):
    tiles = [jnp.int32(0)] * PMAX
    ranks = []
    count = jnp.int32(0)
    for i in range(TR):
        bit = pattern[panel, block * TR + i]
        for j in range(min(i + 1, PMAX)):
            tiles[j] = jnp.where((bit == 1) & (count == j), i, tiles[j])
        ranks.append(jnp.where(bit == 1, count, PMAX))
        count = count + bit
    return tiles, ranks, count


def pick(ranks, tile):
    rank = jnp.int32(PMAX)
    for i in range(TR):
        rank = jnp.where(tile == i, ranks[i], rank)
    return rank


def second_of(panel_one, gathered_first, coupled, inverse):
    held = panel_one.astype(F32) - dot_t(gathered_first, coupled)
    high = held.astype(BF)
    low = (held - high.astype(F32)).astype(BF)
    return dot_t(high, inverse) + dot_t(low, inverse)


def exchange(
    pattern_hbm, panels_hbm, coupling_hbm, inverse_hbm, trailing_hbm,
    own_ref, other_ref, trail_ref,
    pattern, cand, sendbuf, panv, inv, coup, coupled, dland, first, pick_buf,
    local_sem, bsend, brecv, fsend, frecv, dsend, drecv, gsend, grecv, osend,
):
    r = lax.axis_index("row")
    c = lax.axis_index("col")
    z, k = r // 2, r % 2
    zc = c // 2
    sibling = (z * 2 + 1 - k, c)
    half = c % 2

    def plane(i):
        return lax.rem(z + 1 + i, NZ)

    barrier = pltpu.get_barrier_semaphore()

    def greet(device):
        pl.semaphore_signal(barrier, inc=1, device_id=device, device_id_type=MESH)

    greet(sibling)
    for i in range(NZ - 1):
        greet((plane(i) * 2 + k, c))

    @pl.when(z != zc)
    def _():
        for i in range(NP // 2):
            greet((c, 2 * i + k))

    local = [
        pltpu.make_async_copy(pattern_hbm, pattern, local_sem.at[0]),
        pltpu.make_async_copy(
            panels_hbm.at[:, :, pl.ds(pl.multiple_of(16 * (c // 2), 16), 16), pl.ds(pl.multiple_of(256 * half, 256), 256)],
            cand, local_sem.at[1]),
        pltpu.make_async_copy(coupling_hbm, coup.at[pl.ds(pl.multiple_of(32 * r, 32), 32)], local_sem.at[2]),
        pltpu.make_async_copy(panels_hbm, panv, local_sem.at[3]),
        pltpu.make_async_copy(inverse_hbm, inv, local_sem.at[4]),
        pltpu.make_async_copy(trailing_hbm, trail_ref, local_sem.at[5]),
    ]
    for copy in local:
        copy.start()
    pl.semaphore_wait(barrier, 2 * NZ - 1)

    mine = coup.at[pl.ds(pl.multiple_of(32 * r, 32), 32)]
    local[2].wait()
    shard_copies = []
    for i in range(NZ - 1):
        copy = pltpu.make_async_remote_copy(
            src_ref=mine, dst_ref=mine, send_sem=bsend.at[i], recv_sem=brecv.at[NZ - 2 - i],
            device_id=(plane(i) * 2 + k, c), device_id_type=MESH)
        copy.start()
        shard_copies.append(copy)
    own_forward = pltpu.make_async_remote_copy(
        src_ref=mine, dst_ref=mine, send_sem=fsend.at[NZ - 1], recv_sem=frecv.at[NZ - 1],
        device_id=sibling, device_id_type=MESH)
    own_forward.start()

    local[0].wait()
    local[1].wait()
    own_places = [places(pattern, q, r) for q in range(2)]
    for q in range(2):
        tiles, _, count = own_places[q]
        for j in range(PMAX):
            value = cand[q, tiles[j]]
            sendbuf[q, j] = jnp.where(count > j, value, jnp.zeros_like(value))
    piece_rows = pl.ds(pl.multiple_of(16 * (c // 2), 16), 16)
    piece_cols = pl.ds(pl.multiple_of(256 * half, 256), 256)
    piece_copies = []
    for i in range(NZ - 1):
        copy = pltpu.make_async_remote_copy(
            src_ref=sendbuf, dst_ref=dland.at[:, :, piece_rows, piece_cols],
            send_sem=dsend.at[i], recv_sem=drecv.at[c // 2],
            device_id=(plane(i) * 2 + half, r), device_id_type=MESH)
        copy.start()
        piece_copies.append(copy)

    local[3].wait()
    for q in range(2):
        tiles, _, count = own_places[q]
        for j in range(PMAX):
            value = panv[q, tiles[j]]
            pick_buf[q, j] = jnp.where(count > j, value, jnp.zeros_like(value))

    @pl.when(r == c)
    def _():
        dland[...] = pick_buf[...]
        pltpu.make_async_remote_copy(
            src_ref=pick_buf, dst_ref=dland, send_sem=osend.at[0], recv_sem=osend.at[1],
            device_id=sibling, device_id_type=MESH).start()

    local[4].wait()
    first[PMAX] = jnp.zeros((BS, W), BF)
    own_first = dot_t(pick_buf[0].reshape(PMAX * BS, W), inv[0]).astype(BF).reshape(PMAX, BS, W)
    first[:PMAX] = own_first
    own_ref[0] = own_first

    for i in range(NZ - 1):
        shard_copies[NZ - 2 - i].wait_recv()
        there = coup.at[pl.ds(pl.multiple_of(32 * (plane(i) * 2 + k), 32), 32)]
        pltpu.make_async_remote_copy(
            src_ref=there, dst_ref=there, send_sem=fsend.at[i], recv_sem=frecv.at[i],
            device_id=sibling, device_id_type=MESH).start()

    def piece_at(i):
        return dland.at[:, :, pl.ds(16 * i, 16), pl.ds(pl.multiple_of(256 * k, 256), 256)]

    def piece_forward(i):
        return pltpu.make_async_remote_copy(
            src_ref=piece_at(i), dst_ref=piece_at(i), send_sem=gsend.at[i], recv_sem=grecv.at[i],
            device_id=sibling, device_id_type=MESH)

    @pl.when(z != zc)
    def _():
        for i in range(NP // 2):
            pltpu.make_async_remote_copy(
                src_ref=sendbuf, dst_ref=piece_at(i), send_sem=dsend.at[0], recv_sem=drecv.at[i],
                device_id=sibling, device_id_type=MESH).wait_recv()
            piece_forward(i).start()

    for i in range(NZ):
        there = coup.at[pl.ds(pl.multiple_of(32 * (plane(i) * 2 + 1 - k), 32), 32)]
        pltpu.make_async_remote_copy(
            src_ref=there, dst_ref=there, send_sem=fsend.at[i], recv_sem=frecv.at[i],
            device_id=sibling, device_id_type=MESH).wait_recv()
    coupled[...] = dot_t(coup[...], inv[0]).astype(BF)

    def masked_gather(of_places):
        count = of_places[1][2]
        parts = []
        for j in range(PMAX):
            value = first[pick(of_places[0][1], of_places[1][0][j])]
            parts.append(jnp.where(count > j, value, jnp.zeros_like(value)))
        return jnp.concatenate(parts, axis=0)

    own_ref[1] = second_of(
        pick_buf[1].reshape(PMAX * BS, W), masked_gather(own_places), coupled[...], inv[1]
    ).astype(BF).reshape(PMAX, BS, W)

    @pl.when(z != zc)
    def _():
        for i in range(NP // 2):
            pltpu.make_async_remote_copy(
                src_ref=sendbuf, dst_ref=dland.at[:, :, pl.ds(16 * i, 16), pl.ds(pl.multiple_of(256 * (1 - k), 256), 256)],
                send_sem=gsend.at[i], recv_sem=grecv.at[i],
                device_id=sibling, device_id_type=MESH).wait_recv()

    whole = pltpu.make_async_remote_copy(
        src_ref=pick_buf, dst_ref=dland, send_sem=osend.at[0], recv_sem=osend.at[1],
        device_id=sibling, device_id_type=MESH)

    @pl.when((z == zc) & (r != c))
    def _():
        whole.wait_recv()

    other_places = [places(pattern, q, c) for q in range(2)]
    other_first = dot_t(dland[0].reshape(PMAX * BS, W), inv[0]).astype(BF).reshape(PMAX, BS, W)
    first[:PMAX] = other_first
    other_ref[0] = other_first
    other_ref[1] = second_of(
        dland[1].reshape(PMAX * BS, W), masked_gather(other_places), coupled[...], inv[1]
    ).astype(BF).reshape(PMAX, BS, W)

    local[5].wait()
    for copy in shard_copies + piece_copies:
        copy.wait_send()
    own_forward.wait_send()
    for i in range(NZ - 1):
        there = coup.at[pl.ds(pl.multiple_of(32 * (plane(i) * 2 + k), 32), 32)]
        pltpu.make_async_remote_copy(
            src_ref=there, dst_ref=there, send_sem=fsend.at[i], recv_sem=frecv.at[i],
            device_id=sibling, device_id_type=MESH).wait_send()

    @pl.when(z != zc)
    def _():
        for i in range(NP // 2):
            piece_forward(i).wait_send()

    @pl.when(r == c)
    def _():
        whole.wait_send()


def finish(pattern_hbm, own, other, trail, factor_hbm, updated_hbm, pattern, zeros, products, strip, sem):
    r = lax.axis_index("row")
    c = lax.axis_index("col")
    copy = pltpu.make_async_copy(pattern_hbm, pattern, sem.at[0])
    copy.start()
    zeros[...] = jnp.zeros_like(zeros)
    copy.wait()
    own_places = [places(pattern, q, r) for q in range(2)]
    other_places = [places(pattern, q, c) for q in range(2)]

    def strip_rows(i):
        return pl.ds(i * BS, BS)

    empty = [(own_places[0][1][i] == PMAX) & (own_places[1][1][i] == PMAX) for i in range(TR)]
    for i in range(TR):
        @pl.when(empty[i])
        def _():
            pltpu.make_async_copy(trail.at[strip_rows(i)], updated_hbm.at[strip_rows(i)], sem.at[1 + i]).start()
    for q in range(2):
        for i in range(TR):
            rank = own_places[q][1][i]

            @pl.when(rank < PMAX)
            def _():
                pltpu.make_async_copy(own.at[q, rank], factor_hbm.at[q, i], sem.at[9 + q * TR + i]).start()

            @pl.when(rank == PMAX)
            def _():
                pltpu.make_async_copy(zeros, factor_hbm.at[q, i], sem.at[9 + q * TR + i]).start()
    for q in range(2):
        product = dot_t(own[q].reshape(PMAX * BS, W), other[q].reshape(PMAX * BS, W))
        for a in range(PMAX):
            for b in range(PMAX):
                products[q, a, b] = product[a * BS:(a + 1) * BS, b * BS:(b + 1) * BS]
        for a in range(PMAX + 1):
            products[q, a, PMAX] = jnp.zeros((BS, BS), F32)
            products[q, PMAX, a] = jnp.zeros((BS, BS), F32)
    for i in range(TR):
        @pl.when(jnp.logical_not(empty[i]))
        def _():
            for j in range(TR):
                cols = pl.ds(j * BS, BS)
                strip[strip_rows(i), cols] = trail[strip_rows(i), cols] - (
                    products[0, own_places[0][1][i], other_places[0][1][j]]
                    + products[1, own_places[1][1][i], other_places[1][1][j]]
                )
            pltpu.make_async_copy(strip.at[strip_rows(i)], updated_hbm.at[strip_rows(i)], sem.at[1 + i]).start()
    for i in range(TR):
        pltpu.make_async_copy(strip.at[strip_rows(i)], updated_hbm.at[strip_rows(i)], sem.at[1 + i]).wait()
        for q in range(2):
            pltpu.make_async_copy(zeros, factor_hbm.at[q, i], sem.at[9 + q * TR + i]).wait()


def body(panels, row_pattern, coupling, inverse_factors, trailing):
    hbm = pl.BlockSpec(memory_space=pltpu.HBM)
    pin = lambda x: pltpu.with_memory_space_constraint(x, pltpu.HBM)
    vmem = pl.BlockSpec(memory_space=pltpu.VMEM)
    dma = pltpu.SemaphoreType.DMA
    packed = (2, PMAX, BS, W)
    panels4 = pin(panels.reshape(2, TR, BS, W))
    row_pattern, coupling, inverse_factors, trailing = map(pin, (row_pattern, coupling, inverse_factors, trailing))
    own, other, trail = pl.pallas_call(
        exchange,
        out_shape=(
            jax.ShapeDtypeStruct(packed, BF),
            jax.ShapeDtypeStruct(packed, BF),
            jax.ShapeDtypeStruct(trailing.shape, F32),
        ),
        in_specs=[hbm] * 5,
        out_specs=(vmem, vmem, vmem),
        scratch_shapes=[
            pltpu.SMEM((2, 128), jnp.int32),
            pltpu.VMEM((2, TR, 16, 256), BF),
            pltpu.VMEM((2, PMAX, 16, 256), BF),
            pltpu.VMEM((2, TR, BS, W), BF),
            pltpu.VMEM((2, W, W), BF),
            pltpu.VMEM((W, W), BF),
            pltpu.VMEM((W, W), BF),
            pltpu.VMEM(packed, BF),
            pltpu.VMEM((PMAX + 1, BS, W), BF),
            pltpu.VMEM(packed, BF),
            dma((6,)), dma((8,)), dma((8,)), dma((8,)), dma((8,)), dma((8,)), dma((8,)), dma((8,)), dma((8,)), dma((2,)),
        ],
        compiler_params=pltpu.CompilerParams(collective_id=0, has_side_effects=True, vmem_limit_bytes=40 << 20),
        cost_estimate=pl.CostEstimate(flops=4_000_000_000, bytes_accessed=12 << 20, transcendentals=0),
    )(row_pattern, panels4, coupling, inverse_factors, trailing)
    factor, updated = pl.pallas_call(
        finish,
        out_shape=(
            jax.ShapeDtypeStruct((2, TR, BS, W), BF),
            jax.ShapeDtypeStruct(trailing.shape, F32),
        ),
        in_specs=[hbm, vmem, vmem, vmem],
        out_specs=(hbm, hbm),
        scratch_shapes=[
            pltpu.SMEM((2, 128), jnp.int32),
            pltpu.VMEM((BS, W), BF),
            pltpu.VMEM((2, PMAX + 1, PMAX + 1, BS, BS), F32),
            pltpu.VMEM((TR * BS, TR * BS), F32),
            dma((32,)),
        ],
        compiler_params=pltpu.CompilerParams(vmem_limit_bytes=40 << 20),
    )(row_pattern, own, other, trail)
    return factor.reshape(panels.shape), updated


def solution(mesh):
    placed = (P(None, "row", None), P(), P("row", None), P(), P("row", "col"))
    return jax.shard_map(
        body,
        mesh=mesh,
        in_specs=placed,
        out_specs=(P(None, "row", None), P("row", "col")),
        check_vma=False,
    )
```

time: 176 us -> 36.4 us (0.21); the launches traced: 173 us -> 36 us
  waiting for transfers between devices: 114 us -> 0 us
  Pallas kernels: 0 us -> 35.3 us
  blocking collectives: 18.9 us -> 0 us
  between operations: 14.1 us -> 0.64 us
  matrix products: 10.6 us -> 0 us
  other arithmetic: 8.01 us -> 0 us
  local copies, waits for them, and re-layouts: 7.89 us -> 0 us
    psum x1 -> x0, waiting for transfers between devices: 114 us -> none  [spread(): return lax.psum(block, axis)]
    pallas_call x0 -> x2, Pallas kernels: none -> 35.3 us  [the longest x1 31.3 us: body(): pl.pallas_call(exchange, out_shape=(jax.ShapeDtypeStruct(packed, BF), jax...]
    all_gather x1 -> x0, blocking collectives: 18.9 us -> none  [body(): coupled = lax.all_gather(coupled_part, 'row', axis=0, tiled=True)]
    dot_general x5 -> x0, matrix products: 10.6 us -> none  [the longest x1 5.96 us: body(): jnp.einsum('krw,qklcw->rlqc', factor, stacked, preferred_element_type=jnp...]
    reshape x2 -> x0, local copies, waits for them, and re-layouts: 7.02 us -> none  [the longest x1 5.35 us: body(): update = jnp.einsum('krw,qklcw->rlqc', factor, stacked, preferred_element...]
    sub x1 -> x0, other arithmetic: 6.85 us -> none  [body(): result = trailing - update]
  transfers between devices with their start and end apart: 1 -> 0, of which waited for: 1 -> 0; matrix products, arithmetic and copies ran while one was open for 0% -> 0% of each run, Pallas kernels for 0% -> 0%
where the time goes in v1:
time: 36.4 us; the launch traced here: 36 us
  Pallas kernels  35.3 us (97%)
  between operations  0.64 us (2%)
    pallas_call x1, Pallas kernels, body(): pl.pallas_call(exchange, out_shape=(jax.ShapeDtypeStruct(packed, BF), jax...  31.3 us
    pallas_call x1, Pallas kernels, body(): pl.pallas_call(finish, out_shape=(jax.ShapeDtypeStruct((2, TR, BS, W), BF...  4.02 us

profile of v1, /device:TPU:71, one launch (start us, length us, event | category | flops | bytes accessed | tf_op | source)
XLA Modules:
  0.0 36.0 jit_solution(7754548893928950317)
XLA Ops:
  0.6 31.3 %shard_map.68 = (bf16[2,3,128,512]{3,2,1,0:T(8,128)(2,1)S(1)}, bf16[2,3,128,512]{3,2,1,0:T(8,128)(2,1)S(1)}, f32[1024,1024]{1,0:T(8,128)S(1)}) custom-call(s32[2,128]{1,0:T(2,128)} %pattern_hbm.3, bf16[2,8,128,512]{3,2,1,0:T(8,128)(2,1)} %bitcast.2, bf16[32,512]{1,0:T(8,128)(2,1)} %coupling_hbm.1, bf16[2,512,512]{2,1,0:T(8,128)(2,1)} %inverse_hbm.1, ...), custom_call_target="tpu_custom_call" | custom-call | flops 4000000000 | bytes 12582912 | tf_op jit(solution)/shard_map/pallas_call | solution.py:294
  32.0 4.0 %shard_map.69 = (bf16[2,8,128,512]{3,2,1,0:T(8,128)(2,1)}, f32[1024,1024]{1,0:T(8,128)}) custom-call(s32[2,128]{1,0:T(2,128)} %pattern_hbm.3, bf16[2,3,128,512]{3,2,1,0:T(8,128)(2,1)S(1)} %get-tuple-element.7.own, bf16[2,3,128,512]{3,2,1,0:T(8,128)(2,1)S(1)} %get-tuple-element.8.other, f32[1024,1024]{1,0:T(8,128)S(1)} %get-tuple-element.9.trail), custom_call_target="tpu_custom_call" | custom-call | tf_op jit(solution)/shard_map/pallas_call | solution.py:319

commit v2 on v1

--- a/solution.py
+++ b/solution.py
@@ -11,6 +11,7 @@
 PMAX = 3
 NZ = 8
 NP = 16
+NX = 4
 MESH = pl.DeviceIdType.MESH
 BF = jnp.bfloat16
 F32 = jnp.float32
@@ -50,18 +51,23 @@
 def exchange(
     pattern_hbm, panels_hbm, coupling_hbm, inverse_hbm, trailing_hbm,
     own_ref, other_ref, trail_ref,
-    pattern, cand, sendbuf, panv, inv, coup, coupled, dland, first, pick_buf,
-    local_sem, bsend, brecv, fsend, frecv, dsend, drecv, gsend, grecv, osend,
+    pattern, cand, sendbuf, panv, inv, coup, coupled, dland, first, picked,
+    local_sem, bsend, brecv, xsend, xrecv, fsend, frecv, dsend, drecv, gsend, grecv, wsem,
 ):
     r = lax.axis_index("row")
     c = lax.axis_index("col")
     z, k = r // 2, r % 2
+    x, y = c // 4, c % 4
     zc = c // 2
     sibling = (z * 2 + 1 - k, c)
     half = c % 2
 
-    def plane(i):
-        return lax.rem(z + 1 + i, NZ)
+    def remote(src, dst, send, recv, device):
+        return pltpu.make_async_remote_copy(
+            src_ref=src, dst_ref=dst, send_sem=send, recv_sem=recv, device_id=device, device_id_type=MESH)
+
+    def across(d):
+        return lax.rem(x + d, NX)
 
     barrier = pltpu.get_barrier_semaphore()
 
@@ -69,41 +75,48 @@
         pl.semaphore_signal(barrier, inc=1, device_id=device, device_id_type=MESH)
 
     greet(sibling)
-    for i in range(NZ - 1):
-        greet((plane(i) * 2 + k, c))
+    for i in range(1, NZ):
+        greet((lax.rem(z + i, NZ) * 2 + k, c))
+    for d in range(1, NX):
+        greet((r, across(d) * 4 + y))
 
     @pl.when(z != zc)
     def _():
         for i in range(NP // 2):
             greet((c, 2 * i + k))
 
+    piece_rows = pl.ds(pl.multiple_of(16 * (c // 2), 16), 16)
+    piece_cols = pl.ds(pl.multiple_of(256 * half, 256), 256)
+
+    def quarter(d):
+        return pl.ds(pl.multiple_of(128 * across(d), 128), 128)
+
     local = [
         pltpu.make_async_copy(pattern_hbm, pattern, local_sem.at[0]),
-        pltpu.make_async_copy(
-            panels_hbm.at[:, :, pl.ds(pl.multiple_of(16 * (c // 2), 16), 16), pl.ds(pl.multiple_of(256 * half, 256), 256)],
-            cand, local_sem.at[1]),
-        pltpu.make_async_copy(coupling_hbm, coup.at[pl.ds(pl.multiple_of(32 * r, 32), 32)], local_sem.at[2]),
+        pltpu.make_async_copy(panels_hbm.at[:, :, piece_rows, piece_cols], cand, local_sem.at[1]),
+        pltpu.make_async_copy(coupling_hbm.at[:, quarter(0)], coup.at[z, k, :, quarter(0)], local_sem.at[2]),
         pltpu.make_async_copy(panels_hbm, panv, local_sem.at[3]),
         pltpu.make_async_copy(inverse_hbm, inv, local_sem.at[4]),
         pltpu.make_async_copy(trailing_hbm, trail_ref, local_sem.at[5]),
     ]
     for copy in local:
         copy.start()
-    pl.semaphore_wait(barrier, 2 * NZ - 1)
-
-    mine = coup.at[pl.ds(pl.multiple_of(32 * r, 32), 32)]
-    local[2].wait()
-    shard_copies = []
-    for i in range(NZ - 1):
-        copy = pltpu.make_async_remote_copy(
-            src_ref=mine, dst_ref=mine, send_sem=bsend.at[i], recv_sem=brecv.at[NZ - 2 - i],
-            device_id=(plane(i) * 2 + k, c), device_id_type=MESH)
-        copy.start()
-        shard_copies.append(copy)
-    own_forward = pltpu.make_async_remote_copy(
-        src_ref=mine, dst_ref=mine, send_sem=fsend.at[NZ - 1], recv_sem=frecv.at[NZ - 1],
-        device_id=sibling, device_id_type=MESH)
-    own_forward.start()
+    pl.semaphore_wait(barrier, 2 * NZ - 1 + NX - 1)
+
+    def shard(plane):
+        return remote(
+            coupling_hbm.at[:, quarter(0)], coup.at[z, k, :, quarter(0)],
+            bsend.at[plane], brecv.at[z], (plane * 2 + k, c))
+
+    def shard_from(plane):
+        return remote(
+            coupling_hbm.at[:, quarter(0)], coup.at[plane, k, :, quarter(0)],
+            bsend.at[plane], brecv.at[plane], (plane * 2 + k, c))
+
+    for plane in range(NZ):
+        @pl.when(plane != z)
+        def _():
+            shard(plane).start()
 
     local[0].wait()
     local[1].wait()
@@ -113,68 +126,75 @@
         for j in range(PMAX):
             value = cand[q, tiles[j]]
             sendbuf[q, j] = jnp.where(count > j, value, jnp.zeros_like(value))
-    piece_rows = pl.ds(pl.multiple_of(16 * (c // 2), 16), 16)
-    piece_cols = pl.ds(pl.multiple_of(256 * half, 256), 256)
-    piece_copies = []
-    for i in range(NZ - 1):
-        copy = pltpu.make_async_remote_copy(
-            src_ref=sendbuf, dst_ref=dland.at[:, :, piece_rows, piece_cols],
-            send_sem=dsend.at[i], recv_sem=drecv.at[c // 2],
-            device_id=(plane(i) * 2 + half, r), device_id_type=MESH)
-        copy.start()
-        piece_copies.append(copy)
+
+    def piece(plane):
+        return remote(
+            sendbuf, dland.at[:, :, piece_rows, piece_cols],
+            dsend.at[plane], drecv.at[c // 2], (plane * 2 + half, r))
+
+    for d in [1, 7, 2, 6, 3, 5, 4]:
+        piece(lax.rem(z + d, NZ)).start()
 
     local[3].wait()
     for q in range(2):
         tiles, _, count = own_places[q]
         for j in range(PMAX):
             value = panv[q, tiles[j]]
-            pick_buf[q, j] = jnp.where(count > j, value, jnp.zeros_like(value))
+            picked[q, j] = jnp.where(count > j, value, jnp.zeros_like(value))
+    whole = remote(picked, dland, wsem.at[0], wsem.at[1], sibling)
 
     @pl.when(r == c)
     def _():
-        dland[...] = pick_buf[...]
-        pltpu.make_async_remote_copy(
-            src_ref=pick_buf, dst_ref=dland, send_sem=osend.at[0], recv_sem=osend.at[1],
-            device_id=sibling, device_id_type=MESH).start()
+        whole.start()
+        dland[...] = picked[...]
 
     local[4].wait()
     first[PMAX] = jnp.zeros((BS, W), BF)
-    own_first = dot_t(pick_buf[0].reshape(PMAX * BS, W), inv[0]).astype(BF).reshape(PMAX, BS, W)
+    own_first = dot_t(picked[0].reshape(PMAX * BS, W), inv[0]).astype(BF).reshape(PMAX, BS, W)
     first[:PMAX] = own_first
     own_ref[0] = own_first
 
-    for i in range(NZ - 1):
-        shard_copies[NZ - 2 - i].wait_recv()
-        there = coup.at[pl.ds(pl.multiple_of(32 * (plane(i) * 2 + k), 32), 32)]
-        pltpu.make_async_remote_copy(
-            src_ref=there, dst_ref=there, send_sem=fsend.at[i], recv_sem=frecv.at[i],
-            device_id=sibling, device_id_type=MESH).start()
-
-    def piece_at(i):
-        return dland.at[:, :, pl.ds(16 * i, 16), pl.ds(pl.multiple_of(256 * k, 256), 256)]
-
-    def piece_forward(i):
-        return pltpu.make_async_remote_copy(
-            src_ref=piece_at(i), dst_ref=piece_at(i), send_sem=gsend.at[i], recv_sem=grecv.at[i],
-            device_id=sibling, device_id_type=MESH)
+    local[2].wait()
+    for plane in range(NZ):
+        @pl.when(plane != z)
+        def _():
+            shard_from(plane).wait_recv()
+
+    def quarter_block(d, core):
+        return coup.at[:, core, :, quarter(d)]
+
+    def along(d):
+        return remote(
+            quarter_block(0, k), quarter_block(0, k), xsend.at[d], xrecv.at[NX - d], (r, across(d) * 4 + y))
+
+    def quarter_forward(d, core):
+        return remote(
+            quarter_block(d, core), quarter_block(d, core), fsend.at[d], frecv.at[d], sibling)
+
+    for d in range(1, NX):
+        along(d).start()
+    quarter_forward(0, k).start()
+    for d in range(1, NX):
+        remote(quarter_block(d, k), quarter_block(d, k), xsend.at[d], xrecv.at[d], sibling).wait_recv()
+        quarter_forward(d, k).start()
+
+    def piece_at(i, core):
+        return dland.at[:, :, pl.ds(16 * i, 16), pl.ds(pl.multiple_of(256 * core, 256), 256)]
+
+    def piece_forward(i, core):
+        return remote(piece_at(i, core), piece_at(i, core), gsend.at[i], grecv.at[i], sibling)
 
     @pl.when(z != zc)
     def _():
         for i in range(NP // 2):
-            pltpu.make_async_remote_copy(
-                src_ref=sendbuf, dst_ref=piece_at(i), send_sem=dsend.at[0], recv_sem=drecv.at[i],
-                device_id=sibling, device_id_type=MESH).wait_recv()
-            piece_forward(i).start()
-
-    for i in range(NZ):
-        there = coup.at[pl.ds(pl.multiple_of(32 * (plane(i) * 2 + 1 - k), 32), 32)]
-        pltpu.make_async_remote_copy(
-            src_ref=there, dst_ref=there, send_sem=fsend.at[i], recv_sem=frecv.at[i],
-            device_id=sibling, device_id_type=MESH).wait_recv()
-    coupled[...] = dot_t(coup[...], inv[0]).astype(BF)
-
-    def masked_gather(of_places):
+            remote(sendbuf, piece_at(i, k), dsend.at[0], drecv.at[i], sibling).wait_recv()
+            piece_forward(i, k).start()
+
+    for d in range(NX):
+        quarter_forward(d, 1 - k).wait_recv()
+    coupled[...] = dot_t(coup[...].reshape(W, W), inv[0]).astype(BF)
+
+    def matching_first(of_places):
         count = of_places[1][2]
         parts = []
         for j in range(PMAX):
@@ -183,20 +203,13 @@
         return jnp.concatenate(parts, axis=0)
 
     own_ref[1] = second_of(
-        pick_buf[1].reshape(PMAX * BS, W), masked_gather(own_places), coupled[...], inv[1]
+        picked[1].reshape(PMAX * BS, W), matching_first(own_places), coupled[...], inv[1]
     ).astype(BF).reshape(PMAX, BS, W)
 
     @pl.when(z != zc)
     def _():
         for i in range(NP // 2):
-            pltpu.make_async_remote_copy(
-                src_ref=sendbuf, dst_ref=dland.at[:, :, pl.ds(16 * i, 16), pl.ds(pl.multiple_of(256 * (1 - k), 256), 256)],
-                send_sem=gsend.at[i], recv_sem=grecv.at[i],
-                device_id=sibling, device_id_type=MESH).wait_recv()
-
-    whole = pltpu.make_async_remote_copy(
-        src_ref=pick_buf, dst_ref=dland, send_sem=osend.at[0], recv_sem=osend.at[1],
-        device_id=sibling, device_id_type=MESH)
+            piece_forward(i, 1 - k).wait_recv()
 
     @pl.when((z == zc) & (r != c))
     def _():
@@ -207,23 +220,24 @@
     first[:PMAX] = other_first
     other_ref[0] = other_first
     other_ref[1] = second_of(
-        dland[1].reshape(PMAX * BS, W), masked_gather(other_places), coupled[...], inv[1]
+        dland[1].reshape(PMAX * BS, W), matching_first(other_places), coupled[...], inv[1]
     ).astype(BF).reshape(PMAX, BS, W)
 
     local[5].wait()
-    for copy in shard_copies + piece_copies:
-        copy.wait_send()
-    own_forward.wait_send()
-    for i in range(NZ - 1):
-        there = coup.at[pl.ds(pl.multiple_of(32 * (plane(i) * 2 + k), 32), 32)]
-        pltpu.make_async_remote_copy(
-            src_ref=there, dst_ref=there, send_sem=fsend.at[i], recv_sem=frecv.at[i],
-            device_id=sibling, device_id_type=MESH).wait_send()
+    for plane in range(NZ):
+        @pl.when(plane != z)
+        def _():
+            shard(plane).wait_send()
+            piece(plane).wait_send()
+    for d in range(1, NX):
+        along(d).wait_send()
+    for d in range(NX):
+        quarter_forward(d, k).wait_send()
 
     @pl.when(z != zc)
     def _():
         for i in range(NP // 2):
-            piece_forward(i).wait_send()
+            piece_forward(i, k).wait_send()
 
     @pl.when(r == c)
     def _():
@@ -306,12 +320,13 @@
             pltpu.VMEM((2, PMAX, 16, 256), BF),
             pltpu.VMEM((2, TR, BS, W), BF),
             pltpu.VMEM((2, W, W), BF),
-            pltpu.VMEM((W, W), BF),
+            pltpu.VMEM((NZ, 2, 32, W), BF),
             pltpu.VMEM((W, W), BF),
             pltpu.VMEM(packed, BF),
             pltpu.VMEM((PMAX + 1, BS, W), BF),
             pltpu.VMEM(packed, BF),
-            dma((6,)), dma((8,)), dma((8,)), dma((8,)), dma((8,)), dma((8,)), dma((8,)), dma((8,)), dma((8,)), dma((2,)),
+            dma((6,)), dma((NZ,)), dma((NZ,)), dma((NX,)), dma((NX,)), dma((NX,)), dma((NX,)),
+            dma((NZ,)), dma((NP // 2,)), dma((NP // 2,)), dma((NP // 2,)), dma((2,)),
         ],
         compiler_params=pltpu.CompilerParams(collective_id=0, has_side_effects=True, vmem_limit_bytes=40 << 20),
         cost_estimate=pl.CostEstimate(flops=4_000_000_000, bytes_accessed=12 << 20, transcendentals=0),

time: 36.4 us -> 32.1 us (0.88)
  Pallas kernels: 35.3 us -> 31.4 us
    pallas_call x1, Pallas kernels: 31.3 us -> 27.4 us  [body(): pl.pallas_call(exchange, out_shape=(jax.ShapeDtypeStruct(packed, BF), jax...]
where the time goes in v2:
time: 32.1 us; the launch traced here: 32 us
  Pallas kernels  31.4 us (98%)
  between operations  0.64 us (2%)
    pallas_call x1, Pallas kernels, body(): pl.pallas_call(exchange, out_shape=(jax.ShapeDtypeStruct(packed, BF), jax...  27.4 us
    pallas_call x1, Pallas kernels, body(): pl.pallas_call(finish, out_shape=(jax.ShapeDtypeStruct((2, TR, BS, W), BF...  4.03 us

profile of v2, /device:TPU:71, one launch (start us, length us, event | category | flops | bytes accessed | tf_op | source)
XLA Modules:
  0.0 32.0 jit_solution(2460417015377438324)
XLA Ops:
  0.6 27.4 %shard_map.68 = (bf16[2,3,128,512]{3,2,1,0:T(8,128)(2,1)S(1)}, bf16[2,3,128,512]{3,2,1,0:T(8,128)(2,1)S(1)}, f32[1024,1024]{1,0:T(8,128)S(1)}) custom-call(s32[2,128]{1,0:T(2,128)} %pattern_hbm.3, bf16[2,8,128,512]{3,2,1,0:T(8,128)(2,1)} %bitcast.2, bf16[32,512]{1,0:T(8,128)(2,1)} %coupling_hbm.1, bf16[2,512,512]{2,1,0:T(8,128)(2,1)} %inverse_hbm.1, ...), custom_call_target="tpu_custom_call" | custom-call | flops 4000000000 | bytes 12582912 | tf_op jit(solution)/shard_map/pallas_call | solution.py:308
  28.0 4.0 %shard_map.69 = (bf16[2,8,128,512]{3,2,1,0:T(8,128)(2,1)}, f32[1024,1024]{1,0:T(8,128)}) custom-call(s32[2,128]{1,0:T(2,128)} %pattern_hbm.3, bf16[2,3,128,512]{3,2,1,0:T(8,128)(2,1)S(1)} %get-tuple-element.7.own, bf16[2,3,128,512]{3,2,1,0:T(8,128)(2,1)S(1)} %get-tuple-element.8.other, f32[1024,1024]{1,0:T(8,128)S(1)} %get-tuple-element.9.trail), custom_call_target="tpu_custom_call" | custom-call | tf_op jit(solution)/shard_map/pallas_call | solution.py:334

commit v3 on v2

--- a/solution.py
+++ b/solution.py
@@ -52,7 +52,7 @@
     pattern_hbm, panels_hbm, coupling_hbm, inverse_hbm, trailing_hbm,
     own_ref, other_ref, trail_ref,
     pattern, cand, sendbuf, panv, inv, coup, coupled, dland, first, picked,
-    local_sem, bsend, brecv, xsend, xrecv, fsend, frecv, dsend, drecv, gsend, grecv, wsem,
+    local_sem, bsend, brecv, xsend, xrecv, fsend, frecv, dsend, drecv, gsend, grecv, wsem, ready,
 ):
     r = lax.axis_index("row")
     c = lax.axis_index("col")
@@ -80,10 +80,9 @@
     for d in range(1, NX):
         greet((r, across(d) * 4 + y))
 
-    @pl.when(z != zc)
-    def _():
-        for i in range(NP // 2):
-            greet((c, 2 * i + k))
+    @pl.when(r != c)
+    def _():
+        greet((z * 2 + half, r))
 
     piece_rows = pl.ds(pl.multiple_of(16 * (c // 2), 16), 16)
     piece_cols = pl.ds(pl.multiple_of(256 * half, 256), 256)
@@ -101,7 +100,26 @@
     ]
     for copy in local:
         copy.start()
-    pl.semaphore_wait(barrier, 2 * NZ - 1 + NX - 1)
+    near = NZ - 1 + 1 + NX - 1
+    teller = z == zc
+
+    @pl.when(jnp.logical_not(teller))
+    def _():
+        pl.semaphore_wait(barrier, near)
+
+    @pl.when(teller & (r != c))
+    def _():
+        pl.semaphore_wait(barrier, near + NP // 2)
+
+    @pl.when(r == c)
+    def _():
+        pl.semaphore_wait(barrier, near + NP // 2 - 1)
+
+
+    for i in range(NP // 2):
+        @pl.when(teller & ((r != c) | (2 * i + k != c)))
+        def _():
+            pl.semaphore_signal(ready, inc=1, device_id=(c, 2 * i + k), device_id_type=MESH)
 
     def shard(plane):
         return remote(
@@ -132,8 +150,20 @@
             sendbuf, dland.at[:, :, piece_rows, piece_cols],
             dsend.at[plane], drecv.at[c // 2], (plane * 2 + half, r))
 
+    @pl.when(r != c)
+    def _():
+        pl.semaphore_wait(ready, 1)
+
+    for plane in range(4):
+        @pl.when(z >= 4)
+        def _():
+            piece(plane).start()
+
     for d in [1, 7, 2, 6, 3, 5, 4]:
-        piece(lax.rem(z + d, NZ)).start()
+        @pl.when((z < 4) | (lax.rem(z + d, NZ) >= 4))
+        def _():
+            piece(lax.rem(z + d, NZ)).start()
+
 
     local[3].wait()
     for q in range(2):
@@ -148,32 +178,32 @@
         whole.start()
         dland[...] = picked[...]
 
+    local[2].wait()
+    for plane in range(NZ):
+        @pl.when(plane != z)
+        def _():
+            shard_from(plane).wait_recv()
+
+    def quarter_block(d, core):
+        return coup.at[:, core, :, quarter(d)]
+
+    def along(d):
+        return remote(
+            quarter_block(0, k), quarter_block(0, k), xsend.at[d], xrecv.at[NX - d], (r, across(d) * 4 + y))
+
+    def quarter_forward(d, core):
+        return remote(
+            quarter_block(d, core), quarter_block(d, core), fsend.at[d], frecv.at[d], sibling)
+
+    for d in range(1, NX):
+        along(d).start()
+    quarter_forward(0, k).start()
     local[4].wait()
     first[PMAX] = jnp.zeros((BS, W), BF)
     own_first = dot_t(picked[0].reshape(PMAX * BS, W), inv[0]).astype(BF).reshape(PMAX, BS, W)
     first[:PMAX] = own_first
     own_ref[0] = own_first
 
-    local[2].wait()
-    for plane in range(NZ):
-        @pl.when(plane != z)
-        def _():
-            shard_from(plane).wait_recv()
-
-    def quarter_block(d, core):
-        return coup.at[:, core, :, quarter(d)]
-
-    def along(d):
-        return remote(
-            quarter_block(0, k), quarter_block(0, k), xsend.at[d], xrecv.at[NX - d], (r, across(d) * 4 + y))
-
-    def quarter_forward(d, core):
-        return remote(
-            quarter_block(d, core), quarter_block(d, core), fsend.at[d], frecv.at[d], sibling)
-
-    for d in range(1, NX):
-        along(d).start()
-    quarter_forward(0, k).start()
     for d in range(1, NX):
         remote(quarter_block(d, k), quarter_block(d, k), xsend.at[d], xrecv.at[d], sibling).wait_recv()
         quarter_forward(d, k).start()
@@ -326,7 +356,7 @@
             pltpu.VMEM((PMAX + 1, BS, W), BF),
             pltpu.VMEM(packed, BF),
             dma((6,)), dma((NZ,)), dma((NZ,)), dma((NX,)), dma((NX,)), dma((NX,)), dma((NX,)),
-            dma((NZ,)), dma((NP // 2,)), dma((NP // 2,)), dma((NP // 2,)), dma((2,)),
+            dma((NZ,)), dma((NP // 2,)), dma((NP // 2,)), dma((NP // 2,)), dma((2,)), pltpu.SemaphoreType.REGULAR,
         ],
         compiler_params=pltpu.CompilerParams(collective_id=0, has_side_effects=True, vmem_limit_bytes=40 << 20),
         cost_estimate=pl.CostEstimate(flops=4_000_000_000, bytes_accessed=12 << 20, transcendentals=0),

time: 32.1 us -> 31.1 us (0.969)
  Pallas kernels: 31.4 us -> 30.4 us
    pallas_call x1, Pallas kernels: 27.4 us -> 26.4 us  [body(): pl.pallas_call(exchange, out_shape=(jax.ShapeDtypeStruct(packed, BF), jax...]
where the time goes in v3:
time: 31.1 us; the launch traced here: 31 us
  Pallas kernels  30.4 us (98%)
  between operations  0.64 us (2%)
    pallas_call x1, Pallas kernels, body(): pl.pallas_call(exchange, out_shape=(jax.ShapeDtypeStruct(packed, BF), jax...  26.4 us
    pallas_call x1, Pallas kernels, body(): pl.pallas_call(finish, out_shape=(jax.ShapeDtypeStruct((2, TR, BS, W), BF...  4.02 us

profile of v3, /device:TPU:71, one launch (start us, length us, event | category | flops | bytes accessed | tf_op | source)
XLA Modules:
  0.0 31.0 jit_solution(7966160798113987552)
XLA Ops:
  0.6 26.4 %shard_map.68 = (bf16[2,3,128,512]{3,2,1,0:T(8,128)(2,1)S(1)}, bf16[2,3,128,512]{3,2,1,0:T(8,128)(2,1)S(1)}, f32[1024,1024]{1,0:T(8,128)S(1)}) custom-call(s32[2,128]{1,0:T(2,128)} %pattern_hbm.3, bf16[2,8,128,512]{3,2,1,0:T(8,128)(2,1)} %bitcast.2, bf16[32,512]{1,0:T(8,128)(2,1)} %coupling_hbm.1, bf16[2,512,512]{2,1,0:T(8,128)(2,1)} %inverse_hbm.1, ...), custom_call_target="tpu_custom_call" | custom-call | flops 4000000000 | bytes 12582912 | tf_op jit(solution)/shard_map/pallas_call | solution.py:338
  27.0 4.0 %shard_map.69 = (bf16[2,8,128,512]{3,2,1,0:T(8,128)(2,1)}, f32[1024,1024]{1,0:T(8,128)}) custom-call(s32[2,128]{1,0:T(2,128)} %pattern_hbm.3, bf16[2,3,128,512]{3,2,1,0:T(8,128)(2,1)S(1)} %get-tuple-element.7.own, bf16[2,3,128,512]{3,2,1,0:T(8,128)(2,1)S(1)} %get-tuple-element.8.other, f32[1024,1024]{1,0:T(8,128)S(1)} %get-tuple-element.9.trail), custom_call_target="tpu_custom_call" | custom-call | tf_op jit(solution)/shard_map/pallas_call | solution.py:364

commit v4 on v3

--- a/solution.py
+++ b/solution.py
@@ -160,10 +160,14 @@
             piece(plane).start()
 
     for d in [1, 7, 2, 6, 3, 5, 4]:
-        @pl.when((z < 4) | (lax.rem(z + d, NZ) >= 4))
+        @pl.when((z < 4) & (lax.rem(z + d, NZ) < 4))
         def _():
             piece(lax.rem(z + d, NZ)).start()
 
+    for d in [1, 7, 2, 6, 3, 5, 4]:
+        @pl.when(lax.rem(z + d, NZ) >= 4)
+        def _():
+            piece(lax.rem(z + d, NZ)).start()
 
     local[3].wait()
     for q in range(2):

time: 31.1 us -> 31.1 us (level)
  no operation moved by 1% of the time
where the time goes in v4:
time: 31.1 us; the launch traced here: 31 us
  Pallas kernels  30.4 us (98%)
  between operations  0.64 us (2%)
    pallas_call x1, Pallas kernels, body(): pl.pallas_call(exchange, out_shape=(jax.ShapeDtypeStruct(packed, BF), jax...  26.4 us
    pallas_call x1, Pallas kernels, body(): pl.pallas_call(finish, out_shape=(jax.ShapeDtypeStruct((2, TR, BS, W), BF...  4.03 us

profile of v4, /device:TPU:71, one launch (start us, length us, event | category | flops | bytes accessed | tf_op | source)
XLA Modules:
  0.0 31.0 jit_solution(5024616105291724702)
XLA Ops:
  0.6 26.4 %shard_map.68 = (bf16[2,3,128,512]{3,2,1,0:T(8,128)(2,1)S(1)}, bf16[2,3,128,512]{3,2,1,0:T(8,128)(2,1)S(1)}, f32[1024,1024]{1,0:T(8,128)S(1)}) custom-call(s32[2,128]{1,0:T(2,128)} %pattern_hbm.3, bf16[2,8,128,512]{3,2,1,0:T(8,128)(2,1)} %bitcast.2, bf16[32,512]{1,0:T(8,128)(2,1)} %coupling_hbm.1, bf16[2,512,512]{2,1,0:T(8,128)(2,1)} %inverse_hbm.1, ...), custom_call_target="tpu_custom_call" | custom-call | flops 4000000000 | bytes 12582912 | tf_op jit(solution)/shard_map/pallas_call | solution.py:342
  27.0 4.0 %shard_map.69 = (bf16[2,8,128,512]{3,2,1,0:T(8,128)(2,1)}, f32[1024,1024]{1,0:T(8,128)}) custom-call(s32[2,128]{1,0:T(2,128)} %pattern_hbm.3, bf16[2,3,128,512]{3,2,1,0:T(8,128)(2,1)S(1)} %get-tuple-element.7.own, bf16[2,3,128,512]{3,2,1,0:T(8,128)(2,1)S(1)} %get-tuple-element.8.other, f32[1024,1024]{1,0:T(8,128)S(1)} %get-tuple-element.9.trail), custom_call_target="tpu_custom_call" | custom-call | tf_op jit(solution)/shard_map/pallas_call | solution.py:368
